TPU v7x, 32 devices: a whole 2x2x4 slice. The times are simulated.
32 devices in a mesh: cuts: 2 (over y), qa: 16 (over z, x, core).
Axes of the slice: x: 2, y: 2, z: 4, core: 2. Of those that a mesh axis runs over, the one named last changes fastest.
Arguments:
- state: float32 [2, 4194304], P(None, ('cuts', 'qa')), parts along dimension 1, may hold values from -6 to 6
- unitaries: float32 [12, 2, 128, 128], replicated, may hold values from -1 to 1, as said below
- gate_order: int32 [12], replicated, may hold values from 0 to 11, each once
- gate_starts: int32 [12], replicated, may hold values from 0 to 1
- pair_gates: float32 [2, 2, 2, 2], replicated, may hold values from -1 to 1, as said below
Outputs:
- final_state: float32 [2, 4194304], P(None, ('cuts', 'qa')), parts along dimension 1
There are 2 independent parts, one for each index of `cuts`. A program takes and returns all parts, laid end to end along the dimension named above; an argument that names none is the same for every part. Nothing has to cross between parts.
Inputs may be any that keep to these rules, and one draw needn't show every extreme that they name: For every k, unitaries[k, 0] + i unitaries[k, 1] is a unitary matrix. For each p, pair_gates[p, 0] + i pair_gates[p, 1] is a unitary 2 x 2 matrix. `gate_order`: A permutation of 0 .. 11.
All inputs are finite; a program needn't handle non-finite values.
Results may differ from a plain program's by a relative error of at most 0.0003.
Values sent between devices are 32-bit elements; how exact they have to be, the bound alone decides.
A program may use at most 64 MiB of HBM per device.

v0:
```python
from functools import partial

import jax
import jax.numpy as jnp
from jax import lax
from jax.sharding import PartitionSpec as P

HIGH = lax.Precision.HIGHEST


def mix(mat, vec):
    return jnp.einsum("ij,ajb->aib", mat, vec, precision=HIGH)


def dense_branch(re_part, im_part, u_re, u_im, offset):
    gdim = u_re.shape[0]
    gq = gdim.bit_length() - 1
    block = 2 ** (gq + offset)
    shaped_re = re_part.reshape(-1, gdim, block)
    shaped_im = im_part.reshape(-1, gdim, block)
    new_re = mix(u_re, shaped_re) - mix(u_im, shaped_im)
    new_im = mix(u_re, shaped_im) + mix(u_im, shaped_re)
    return (new_re.reshape(-1), new_im.reshape(-1))


def dense_gate(stacked, unitaries, gate_order, gate_starts, k):
    chosen = unitaries[gate_order[k]]
    branches = [partial(dense_branch, offset=0), partial(dense_branch, offset=1)]
    new_re, new_im = lax.switch(
        gate_starts[k], branches, stacked[0], stacked[1], chosen[0], chosen[1]
    )
    return jnp.stack([new_re, new_im])


def one_qubit(stacked, gate, qubit):
    shaped = stacked.reshape(2, -1, 2, 2**qubit)
    u_re, u_im = (gate[0], gate[1])
    new_re = jnp.einsum("bc,acx->abx", u_re, shaped[0], precision=HIGH) - jnp.einsum(
        "bc,acx->abx", u_im, shaped[1], precision=HIGH
    )
    new_im = jnp.einsum("bc,acx->abx", u_re, shaped[1], precision=HIGH) + jnp.einsum(
        "bc,acx->abx", u_im, shaped[0], precision=HIGH
    )
    return jnp.stack([new_re, new_im]).reshape(2, -1)


def swap_qubits(stacked):
    devices = lax.axis_size("qa")
    shaped = stacked.reshape(2, devices, -1)
    moved = lax.all_to_all(shaped, "qa", split_axis=1, concat_axis=1, tiled=True)
    return moved.reshape(2, -1)


def shards(state, unitaries, gate_order, gate_starts, pair_gates):
    amp_local = state.shape[1]
    local_bits = amp_local.bit_length() - 1
    global_bits = lax.axis_size("qa").bit_length() - 1
    ngates = unitaries.shape[0]
    third = ngates // 3
    stacked = state
    for k in range(third):
        stacked = dense_gate(stacked, unitaries, gate_order, gate_starts, k)
    stacked = one_qubit(stacked, pair_gates[0], local_bits - 1)
    stacked = swap_qubits(stacked)
    for k in range(third, 2 * third):
        stacked = dense_gate(stacked, unitaries, gate_order, gate_starts, k)
    stacked = one_qubit(stacked, pair_gates[1], local_bits - global_bits)
    stacked = swap_qubits(stacked)
    for k in range(2 * third, ngates):
        stacked = dense_gate(stacked, unitaries, gate_order, gate_starts, k)
    return stacked


def solution(mesh):
    placed = (P(None, ("cuts", "qa")), P(), P(), P(), P())
    return jax.shard_map(
        shards, mesh=mesh, in_specs=placed, out_specs=P(None, ("cuts", "qa")), check_vma=False
    )
```

profile of v0, /device:TPU:15, one launch (start us, length us, event | category | flops | bytes accessed | tf_op | source)
XLA Modules:
  0.0 221.6 jit_solution(4643017972225681178)
XLA Ops:
  0.0 1.8 fusion.243
  16.6 1.8 fusion.244
  21.0 2.5 %fusion.242 = (f32[1,131072]{1,0:T(1,128)S(1)}, f32[1,131072]{1,0:T(1,128)S(1)}) fusion(f32[2,131072]{1,0:T(2,128)} %param.29), kind=kLoop, calls=%fused_computation.318 | loop fusion | bytes 2097152 | tf_op jit(solution)/shard_map/slice | solution.py:30
  29.0 2.1 dynamic-slice_bitcast_fusion
  31.1 9.8 %conditional.12 = (f32[131072]{0:T(1024)S(1)}, f32[131072]{0:T(1024)S(1)}) conditional(s32[]{:T(128)} %bitcast.175, (f32[1,131072]{1,0:T(1,128)S(1)}, f32[128,128]{1,0:T(8,128)S(1)}, f32[1,131072]{1,0:T(1,128)S(1)}, f32[128,128]{1,0:T(8,128)S(1)}) %tuple.113, (f32[1,131072]{1,0:T(1,128)S(1)}, f32[128,128]{1,0:T(8,128)S(1)}, ...), branch_computations={%region_0.0_spmd, %region_1.0_spmd} | conditional | flops 805568512 | bytes 13893664 | solution.py:29
  31.9 1.9 reduce.18
  34.9 1.9 reduce.19
  39.4 1.0 fusion.192
  40.9 4.8 %conditional.13 = (f32[131072]{0:T(1024)S(1)}, f32[131072]{0:T(1024)S(1)}) conditional(s32[]{:T(128)} %bitcast.174, (f32[131072]{0:T(1024)S(1)}, f32[128,128]{1,0:T(8,128)S(1)}, f32[131072]{0:T(1024)S(1)}, f32[128,128]{1,0:T(8,128)S(1)}) %tuple.114, (f32[131072]{0:T(1024)S(1)}, f32[128,128]{1,0:T(8,128)S(1)}, f32[131072]{0:T(1024)S(1)}, ...), branch_computations={%region_2.0_spmd, %region_3.0_spmd} | conditional | flops 805568512 | bytes 11796496 | solution.py:29
  44.1 1.0 fusion.8
  45.7 16.7 %conditional.14 = (f32[131072]{0:T(1024)S(1)}, f32[131072]{0:T(1024)S(1)}) conditional(s32[]{:T(128)} %bitcast.173, (f32[131072]{0:T(1024)S(1)}, f32[128,128]{1,0:T(8,128)S(1)}, f32[131072]{0:T(1024)S(1)}, f32[128,128]{1,0:T(8,128)S(1)}) %tuple.115, (f32[131072]{0:T(1024)S(1)}, f32[128,128]{1,0:T(8,128)S(1)}, f32[131072]{0:T(1024)S(1)}, ...), branch_computations={%region_4.0_spmd, %region_5.0_spmd} | conditional | flops 805568512 | bytes 12845184 | solution.py:29
  57.6 1.9 fusion.33
  64.3 1.1 constant_dynamic-slice_fusion
  65.4 5.9 %conditional.15 = (f32[2,65536]{1,0:T(2,128)S(1)}, f32[2,65536]{1,0:T(2,128)S(1)}) conditional(s32[]{:T(128)} %bitcast.172, (f32[131072]{0:T(1024)S(1)}, f32[1,2,128,128]{3,2,1,0:T(8,128)S(1)}, f32[131072]{0:T(1024)S(1)}) %tuple.116, (f32[131072]{0:T(1024)S(1)}, f32[1,2,128,128]{3,2,1,0:T(8,128)S(1)}, f32[131072]{0:T(1024)S(1)}) %tuple.116), branch_computations={%region_6.0_spmd, %region_7.0_spmd} | conditional | flops 805568512 | bytes 11796496 | solution.py:29
  71.3 1.9 fusion.228
  73.2 1.9 fusion.230
  75.1 1.9 fusion.217
  77.9 1.9 fusion.216
  80.6 1.9 pad_maximum_fusion
  82.6 6.6 %all-to-all-start = ((f32[2,16,8192]{2,0,1:T(2,128)}), f32[2,16,8192]{2,0,1:T(2,128)S(1)}, u32[]{:S(2)}, u32[]{:S(2)}) async-start(f32[2,16,8192]{2,0,1:T(2,128)} %pad_maximum_fusion), calls=%async_computation | async-start | bytes 2097152 | tf_op jit(solution)/shard_map/all_to_all | solution.py:50
  91.6 22.4 %all-to-all-done = f32[2,16,8192]{2,0,1:T(2,128)S(1)} async-done(((f32[2,16,8192]{2,0,1:T(2,128)}), f32[2,16,8192]{2,0,1:T(2,128)S(1)}, u32[]{:S(2)}, u32[]{:S(2)}) %all-to-all-start) | async-done | bytes 1048608 | tf_op jit(solution)/shard_map/all_to_all | solution.py:50
  114.0 1.1 fusion.241
  115.2 9.8 %conditional.16 = (f32[131072]{0:T(1024)S(1)}, f32[131072]{0:T(1024)S(1)}) conditional(s32[]{:T(128)} %bitcast.171, (f32[1,131072]{1,0:T(1,128)S(1)}, f32[128,128]{1,0:T(8,128)S(1)}, f32[1,131072]{1,0:T(1,128)S(1)}, f32[128,128]{1,0:T(8,128)S(1)}) %tuple.211, (f32[1,131072]{1,0:T(1,128)S(1)}, f32[128,128]{1,0:T(8,128)S(1)}, ...), branch_computations={%region_8.0_spmd, %region_9.0_spmd} | conditional | flops 805568512 | bytes 13893664 | solution.py:29
  115.9 1.9 reduce.20
  118.9 1.9 reduce.21
  123.4 1.0 fusion.200
  125.0 4.6 %conditional.17 = (f32[131072]{0:T(1024)S(1)}, f32[131072]{0:T(1024)S(1)}) conditional(s32[]{:T(128)} %bitcast.170, (f32[131072]{0:T(1024)S(1)}, f32[128,128]{1,0:T(8,128)S(1)}, f32[131072]{0:T(1024)S(1)}, f32[128,128]{1,0:T(8,128)S(1)}) %tuple.207, (f32[131072]{0:T(1024)S(1)}, f32[128,128]{1,0:T(8,128)S(1)}, f32[131072]{0:T(1024)S(1)}, ...), branch_computations={%region_10.0_spmd, %region_11.0_spmd} | conditional | flops 805568512 | bytes 11796496 | solution.py:29
  126.2 1.0 fusion.73
  128.4 1.0 fusion.72
  129.6 7.9 %conditional.18 = (f32[131072]{0:T(1024)S(1)}, f32[131072]{0:T(1024)S(1)}) conditional(s32[]{:T(128)} %bitcast.169, (f32[131072]{0:T(1024)S(1)}, f32[128,128]{1,0:T(8,128)S(1)}, f32[131072]{0:T(1024)S(1)}, f32[128,128]{1,0:T(8,128)S(1)}) %tuple.119, (f32[131072]{0:T(1024)S(1)}, f32[128,128]{1,0:T(8,128)S(1)}, f32[131072]{0:T(1024)S(1)}, ...), branch_computations={%region_12.0_spmd, %region_13.0_spmd} | conditional | flops 805568512 | bytes 11796496 | solution.py:29
  137.5 10.5 %conditional.19 = (f32[8,2,8192]{2,1,0:T(2,128)S(1)}, f32[8,2,8192]{2,1,0:T(2,128)S(1)}) conditional(s32[]{:T(128)} %bitcast.168, (f32[131072]{0:T(1024)S(1)}, f32[1,2,128,128]{3,2,1,0:T(8,128)S(1)}, f32[131072]{0:T(1024)S(1)}) %tuple.120, (f32[131072]{0:T(1024)S(1)}, f32[1,2,128,128]{3,2,1,0:T(8,128)S(1)}, f32[131072]{0:T(1024)S(1)}) %tuple.120), branch_computations={%region_14.0_spmd, %region_15.0_spmd} | conditional | flops 805568512 | bytes 11796496 | solution.py:29
  147.9 1.9 fusion.222
  149.8 1.9 fusion.224
  151.8 2.0 fusion.218
  154.5 2.0 fusion.219
  157.3 1.9 pad_maximum_fusion.1
  159.2 4.9 %all-to-all-start.1 = ((f32[2,16,8192]{2,0,1:T(2,128)}), f32[2,16,8192]{2,0,1:T(2,128)S(1)}, u32[]{:S(2)}, u32[]{:S(2)}) async-start(f32[2,16,8192]{2,0,1:T(2,128)} %pad_maximum_fusion.1), calls=%async_computation.1 | async-start | bytes 2097152 | tf_op jit(solution)/shard_map/all_to_all | solution.py:50
  166.7 22.4 %all-to-all-done.1 = f32[2,16,8192]{2,0,1:T(2,128)S(1)} async-done(((f32[2,16,8192]{2,0,1:T(2,128)}), f32[2,16,8192]{2,0,1:T(2,128)S(1)}, u32[]{:S(2)}, u32[]{:S(2)}) %all-to-all-start.1) | async-done | bytes 1048608 | tf_op jit(solution)/shard_map/all_to_all | solution.py:50
  189.1 1.1 fusion.240
  190.2 10.0 %conditional.20 = (f32[131072]{0:T(1024)S(1)}, f32[131072]{0:T(1024)S(1)}) conditional(s32[]{:T(128)} %bitcast.167, (f32[1,131072]{1,0:T(1,128)S(1)}, f32[128,128]{1,0:T(8,128)S(1)}, f32[1,131072]{1,0:T(1,128)S(1)}, f32[128,128]{1,0:T(8,128)S(1)}) %tuple.199, (f32[1,131072]{1,0:T(1,128)S(1)}, f32[128,128]{1,0:T(8,128)S(1)}, ...), branch_computations={%region_16.0_spmd, %region_17.0_spmd} | conditional | flops 805568512 | bytes 13893664 | solution.py:29
  191.1 1.9 reduce.22
  194.2 1.9 reduce.23
  198.7 1.0 fusion.208
  200.2 5.5 %conditional.21 = (f32[131072]{0:T(1024)S(1)}, f32[131072]{0:T(1024)S(1)}) conditional(s32[]{:T(128)} %bitcast.166, (f32[131072]{0:T(1024)S(1)}, f32[128,128]{1,0:T(8,128)S(1)}, f32[131072]{0:T(1024)S(1)}, f32[128,128]{1,0:T(8,128)S(1)}) %tuple.203, (f32[131072]{0:T(1024)S(1)}, f32[128,128]{1,0:T(8,128)S(1)}, f32[131072]{0:T(1024)S(1)}, ...), branch_computations={%region_18.0_spmd, %region_19.0_spmd} | conditional | flops 805568512 | bytes 11796496 | solution.py:29
  205.7 5.9 %conditional.22 = (f32[131072]{0:T(1024)S(1)}, f32[131072]{0:T(1024)S(1)}) conditional(s32[]{:T(128)} %bitcast.165, (f32[131072]{0:T(1024)S(1)}, f32[128,128]{1,0:T(8,128)S(1)}, f32[131072]{0:T(1024)S(1)}, f32[128,128]{1,0:T(8,128)S(1)}) %tuple.123, (f32[131072]{0:T(1024)S(1)}, f32[128,128]{1,0:T(8,128)S(1)}, f32[131072]{0:T(1024)S(1)}, ...), branch_computations={%region_20.0_spmd, %region_21.0_spmd} | conditional | flops 805568512 | bytes 11796496 | solution.py:29
  210.4 1.0 fusion.152
  211.6 7.8 %conditional.23 = (f32[1,131072]{1,0:T(1,128)S(1)}, f32[1,131072]{1,0:T(1,128)S(1)}) conditional(s32[]{:T(128)} %bitcast.164, (f32[131072]{0:T(1024)S(1)}, f32[1,2,128,128]{3,2,1,0:T(8,128)S(1)}, f32[131072]{0:T(1024)S(1)}) %tuple.124, (f32[131072]{0:T(1024)S(1)}, f32[1,2,128,128]{3,2,1,0:T(8,128)S(1)}, f32[131072]{0:T(1024)S(1)}) %tuple.124), branch_computations={%region_22.0_spmd, %region_23.0_spmd} | conditional | flops 805568512 | bytes 11796496 | solution.py:29
  219.4 1.9 pad_maximum_fusion.2
  (125 shorter events, 56.3 us)
Async XLA Ops:
  56.2 1.3 copy-start.6
  56.2 1.3 copy-start.8
  57.6 2.4 %copy-start.7 = (f32[128,128]{1,0:T(8,128)S(1)}, f32[128,128]{1,0:T(8,128)}, u32[]{:S(2)}) copy-start(f32[128,128]{1,0:T(8,128)} %copy-done.6) | copy-start | bytes 196612 | tf_op jit(solution)/shard_map/cond
  59.5 1.5 copy-start.9
  65.4 5.9 %copy-start.10 = (f32[2,2,2,2]{3,2,1,0:T(2,128)S(1)}, f32[2,2,2,2]{3,2,1,0:T(2,128)}, u32[]{:S(2)}) copy-start(f32[2,2,2,2]{3,2,1,0:T(2,128)} %param.33) | copy-start | bytes 196
  82.6 31.4 %all-to-all-start = ((f32[2,16,8192]{2,0,1:T(2,128)}), f32[2,16,8192]{2,0,1:T(2,128)S(1)}, u32[]{:S(2)}, u32[]{:S(2)}) async-start(f32[2,16,8192]{2,0,1:T(2,128)} %pad_maximum_fusion), calls=%async_computation | async-start | bytes 2097152 | tf_op jit(solution)/shard_map/all_to_all | solution.py:50
  89.1 26.0 %copy-start.4 = (f32[128,128]{1,0:T(8,128)S(1)}, f32[128,128]{1,0:T(8,128)}, u32[]{:S(2)}) copy-start(f32[128,128]{1,0:T(8,128)} %get-tuple-element.368) | copy-start | bytes 196612
  89.1 26.0 %copy-start.5 = (f32[128,128]{1,0:T(8,128)S(1)}, f32[128,128]{1,0:T(8,128)}, u32[]{:S(2)}) copy-start(f32[128,128]{1,0:T(8,128)} %get-tuple-element.376) | copy-start | bytes 196612
  115.1 9.8 %copy-start.2 = (f32[128,128]{1,0:T(8,128)S(1)}, f32[128,128]{1,0:T(8,128)}, u32[]{:S(2)}) copy-start(f32[128,128]{1,0:T(8,128)} %get-tuple-element.367) | copy-start | bytes 196612
  115.1 9.8 %copy-start.3 = (f32[128,128]{1,0:T(8,128)S(1)}, f32[128,128]{1,0:T(8,128)}, u32[]{:S(2)}) copy-start(f32[128,128]{1,0:T(8,128)} %get-tuple-element.375) | copy-start | bytes 196612
  159.2 29.8 %all-to-all-start.1 = ((f32[2,16,8192]{2,0,1:T(2,128)}), f32[2,16,8192]{2,0,1:T(2,128)S(1)}, u32[]{:S(2)}, u32[]{:S(2)}) async-start(f32[2,16,8192]{2,0,1:T(2,128)} %pad_maximum_fusion.1), calls=%async_computation.1 | async-start | bytes 2097152 | tf_op jit(solution)/shard_map/all_to_all | solution.py:50
  190.2 10.0 %copy-start = (f32[128,128]{1,0:T(8,128)S(1)}, f32[128,128]{1,0:T(8,128)}, u32[]{:S(2)}) copy-start(f32[128,128]{1,0:T(8,128)} %get-tuple-element.364) | copy-start | bytes 196612
  190.2 10.0 %copy-start.1 = (f32[128,128]{1,0:T(8,128)S(1)}, f32[128,128]{1,0:T(8,128)}, u32[]{:S(2)}) copy-start(f32[128,128]{1,0:T(8,128)} %get-tuple-element.372) | copy-start | bytes 196612
where the time goes:
time: 226 us; the launch traced here: 222 us
  matrix products  63.9 us (28%)
  waiting for transfers between devices  44.7 us (20%)
  between operations  30.4 us (13%)
  local copies, waits for them, and re-layouts  28.1 us (12%)
  loops' own time  26 us (12%)
  other arithmetic  17 us (8%)
  starting transfers between devices  11.5 us (5%)
    dot_general x48, matrix products, mix(): return jnp.einsum('ij,ajb->aib', mat, vec, precision=HIGH)  48.5 us
    all_to_all x2, waiting for transfers between devices, swap_qubits(): lax.all_to_all(shaped, 'qa', split_axis=1, concat_axis=1, tiled=True)  44.7 us
    another operation x12, loops' own time, dense_gate(): lax.switch(gate_starts[k], branches, stacked[0], stacked[1], chosen[0], c...  26 us
    all_to_all x2, starting transfers between devices, swap_qubits(): lax.all_to_all(shaped, 'qa', split_axis=1, concat_axis=1, tiled=True)  11.5 us
    another operation x6, other arithmetic  11.3 us
    slice x3, local copies, waits for them, and re-layouts, dense_gate(): stacked[1]  4.72 us
  transfers between devices with their start and end apart: 2, of which 2 were waited for; matrix products, arithmetic and copies ran while one was open for 0% of the time, Pallas kernels for 0%

commit v1 on v0

v1 whole, which is shorter than its diff:
```python
import functools

import jax
import jax.numpy as jnp
from jax import lax
from jax.experimental import pallas as pl
from jax.experimental.pallas import tpu as pltpu
from jax.sharding import PartitionSpec as P

BF16 = jnp.bfloat16
F32 = jnp.float32


def split(x):
    hi = x.astype(BF16)
    return hi, (x - hi.astype(F32)).astype(BF16)


def dot(a, b):
    return jnp.dot(a, b, preferred_element_type=F32)


def embed(re, im):
    return jnp.concatenate(
        [jnp.concatenate([re, -im], axis=1), jnp.concatenate([im, re], axis=1)], axis=0
    )


def gate_matrix(u, order, k):
    re_hi, re_lo = split(u[order[k], 0])
    im_hi, im_lo = split(u[order[k], 1])
    return embed(re_hi, im_hi), embed(re_lo, im_lo)


def product(mat, x):
    hi, lo = mat
    x_hi, x_lo = split(x)
    return dot(hi, x_hi) + dot(hi, x_lo) + dot(lo, x_hi)


def relayout(y, plain, woven, old, new):
    gdim, lanes = y.shape[0] // 2, y.shape[1] // 2
    parts = [
        [y[r * gdim : (r + 1) * gdim, b * lanes : (b + 1) * lanes] for b in range(2)]
        for r in range(2)
    ]
    for r in range(2):
        for b in range(2):
            plain[r, b * gdim : (b + 1) * gdim, :] = parts[r][b]
            woven[r, pl.ds(b, gdim, stride=2), :] = parts[r][b]
    rows = []
    for r in range(2):
        cols = []
        for b in range(2):
            to_low = woven[r, b * gdim : (b + 1) * gdim, :]
            to_high = plain[r, pl.ds(b, gdim, stride=2), :]
            moved = jnp.where(old == 1, to_low, to_high)
            cols.append(jnp.where(old == new, parts[r][b], moved))
        rows.append(jnp.concatenate(cols, axis=1))
    return jnp.concatenate(rows, axis=0)


def run_gates(planes, mats, marks, plain, woven):
    gdim = planes[0].shape[0] // 2
    y = jnp.concatenate(
        [jnp.concatenate([p[:gdim], p[gdim:]], axis=1) for p in planes], axis=0
    )
    old = jnp.int32(0)
    for mat, new in zip(mats, marks):
        y = product(mat(), relayout(y, plain, woven, old, new))
        old = new
    y = relayout(y, plain, woven, old, jnp.int32(0))
    lanes = y.shape[1] // 2
    return [
        jnp.concatenate(
            [y[r * gdim : (r + 1) * gdim, :lanes], y[r * gdim : (r + 1) * gdim, lanes:]],
            axis=0,
        )
        for r in range(2)
    ]


def mix_pair(pair, p, b, low, high):
    r0, i0 = pair[p, 0, b, 0], pair[p, 1, b, 0]
    r1, i1 = pair[p, 0, b, 1], pair[p, 1, b, 1]
    re = r0 * low[0] - i0 * low[1] + (r1 * high[0] - i1 * high[1])
    im = r0 * low[1] + i0 * low[0] + (r1 * high[1] + i1 * high[0])
    return re, im


def compose(third, count, order, starts, u, plain, woven, w_hi, w_lo, after):
    rows, lanes = plain.shape[1], plain.shape[2]
    ks = [third * count + j for j in range(count)]
    built = [gate_matrix(u, order, k) for k in ks]
    for n in range(rows // lanes):
        at = lax.broadcasted_iota(jnp.int32, (rows, lanes), 0)
        col = lax.broadcasted_iota(jnp.int32, (rows, lanes), 1) + n * lanes
        one = jnp.where(at == col, 1.0, 0.0).astype(F32)
        planes = run_gates(
            [one, jnp.zeros_like(one)],
            [lambda m=m: m for m in built],
            [starts[k] for k in ks],
            plain,
            woven,
        )
        re, im = after(planes)
        for out, r, i in zip((w_hi, w_lo), split(re), split(im)):
            here = slice(n * lanes, (n + 1) * lanes)
            there = slice(rows + n * lanes, rows + (n + 1) * lanes)
            out[:rows, here] = r
            out[rows:, there] = r
            out[rows:, here] = i
            out[:rows, there] = -i


def apply(w_hi, w_lo, x):
    lanes = x.shape[1]
    x_hi, x_lo = split(x)
    both = dot(w_hi[...], jnp.concatenate([x_hi, x_lo], axis=1))
    return both[:, :lanes] + both[:, lanes:] + dot(w_lo[...], x_hi)


def kernel(
    group, pair_bit, order, starts, pair, x_hbm, u_hbm, o_hbm,
    x_in, u, first_hi, first_lo, plain, woven, w_hi, w_lo,
    sent, got, x_out, in_sem, out_sem, send_sem, recv_sem,
):
    chunks, rows, lanes = x_in.shape[0], x_in.shape[1] // 2, x_in.shape[2]
    count = u.shape[0] // 3
    block = rows // group
    index = lax.axis_index("qa")
    me = lax.rem(index, group)
    base = index - me

    barrier = pltpu.get_barrier_semaphore()
    for d in range(1, group):
        pl.semaphore_signal(
            barrier, inc=1, device_id={"qa": base + lax.rem(me + d, group)},
            device_id_type=pl.DeviceIdType.MESH,
        )
    load_u = pltpu.make_async_copy(u_hbm, u, in_sem.at[0])
    load_x = pltpu.make_async_copy(x_hbm, x_in, in_sem.at[1])
    load_u.start()
    load_x.start()
    load_u.wait()
    for k in range(count):
        first_hi[k], first_lo[k] = gate_matrix(u, order, k)
    load_x.wait()

    def block_at(j):
        return pl.ds(pl.multiple_of(j * block, block), block)

    def remote(phase, c, d):
        peer = lax.rem(me + d, group)
        return pltpu.make_async_remote_copy(
            src_ref=sent.at[phase, c, :, block_at(peer), :],
            dst_ref=got.at[phase, c, :, block_at(me), :],
            send_sem=send_sem.at[phase, c, d],
            recv_sem=recv_sem.at[phase, c, d],
            device_id={"qa": base + peer},
            device_id_type=pl.DeviceIdType.MESH,
        )

    def exchange(phase, c):
        def one(d, _):
            remote(phase, c, d).start()
            return 0

        lax.fori_loop(1, group, one, 0)
        got[phase, c, :, block_at(me), :] = sent[phase, c, :, block_at(me), :]

    def arrived(phase, c):
        def one(d, _):
            remote(phase, c, d).wait_recv()
            return 0

        lax.fori_loop(1, group, one, 0)

    def first_gates(c):
        half = chunks // 2
        low, high = lax.rem(c, half), lax.rem(c, half) + half

        def planes_of(n):
            return [x_in[n, pl.ds(r, rows, stride=2), :] for r in range(2)]

        planes = mix_pair(pair, 0, c // half, planes_of(low), planes_of(high))
        done = run_gates(
            planes,
            [lambda k=k: (first_hi[k], first_lo[k]) for k in range(count)],
            [starts[k] for k in range(count)],
            plain,
            woven,
        )
        for r in range(2):
            sent[0, c, r] = done[r]

    first_gates(jnp.int32(0))
    pl.semaphore_wait(barrier, group - 1)
    exchange(0, jnp.int32(0))

    def first(c, _):
        first_gates(c)
        exchange(0, c)
        return 0

    lax.fori_loop(1, chunks, first, 0)

    def with_pair(planes):
        pieces = ([], [])
        for start in range(0, rows, 2 * pair_bit):
            low = [p[start : start + pair_bit] for p in planes]
            high = [p[start + pair_bit : start + 2 * pair_bit] for p in planes]
            for b in range(2):
                for out, part in zip(pieces, mix_pair(pair, 1, b, low, high)):
                    out.append(part)
        return [jnp.concatenate(p, axis=0) for p in pieces]

    compose(1, count, order, starts, u, plain, woven, w_hi, w_lo, with_pair)

    def second(c, _):
        arrived(0, c)
        y = apply(w_hi, w_lo, got[0, c].reshape(2 * rows, lanes))
        sent[1, c] = y.reshape(2, rows, lanes)
        exchange(1, c)
        return 0

    lax.fori_loop(0, chunks, second, 0)

    compose(2, count, order, starts, u, plain, woven, w_hi, w_lo, lambda p: p)

    def store(c):
        return pltpu.make_async_copy(x_out.at[c], o_hbm.at[c], out_sem.at[c])

    def last(c, _):
        arrived(1, c)
        y = apply(w_hi, w_lo, got[1, c].reshape(2 * rows, lanes))
        for r in range(2):
            x_out[c, pl.ds(r, rows, stride=2), :] = y[r * rows : (r + 1) * rows]
        store(c).start()
        return 0

    lax.fori_loop(0, chunks, last, 0)

    def finish(c, _):
        store(c).wait()
        for phase in range(2):
            lax.fori_loop(
                1, group, lambda d, _: (remote(phase, c, d).wait_send(), 0)[1], 0
            )
        return 0

    lax.fori_loop(0, chunks, finish, 0)


def shards(state, unitaries, gate_order, gate_starts, pair_gates):
    amp_local = state.shape[1]
    gdim = unitaries.shape[-1]
    ngates = unitaries.shape[0]
    rows, lanes = 2 * gdim, gdim
    chunks = amp_local // (rows * lanes)
    unit = amp_local // lax.axis_size("qa")
    group = rows * lanes // unit
    x = state.reshape(2, chunks * rows, lanes).transpose(1, 0, 2)
    x = x.reshape(chunks, 2 * rows, lanes)
    smem = pl.BlockSpec(memory_space=pltpu.SMEM)
    hbm = pl.BlockSpec(memory_space=pl.ANY)
    y = pl.pallas_call(
        functools.partial(kernel, group, unit // lanes),
        out_shape=jax.ShapeDtypeStruct(x.shape, F32),
        in_specs=[smem, smem, smem, hbm, hbm],
        out_specs=hbm,
        scratch_shapes=[
            pltpu.VMEM(x.shape, F32),
            pltpu.VMEM(unitaries.shape, F32),
            pltpu.VMEM((ngates // 3, 2 * gdim, 2 * gdim), BF16),
            pltpu.VMEM((ngates // 3, 2 * gdim, 2 * gdim), BF16),
            pltpu.VMEM((2, rows, lanes), F32),
            pltpu.VMEM((2, rows, lanes), F32),
            pltpu.VMEM((2 * rows, 2 * rows), BF16),
            pltpu.VMEM((2 * rows, 2 * rows), BF16),
            pltpu.VMEM((2, chunks, 2, rows, lanes), F32),
            pltpu.VMEM((2, chunks, 2, rows, lanes), F32),
            pltpu.VMEM(x.shape, F32),
            pltpu.SemaphoreType.DMA((2,)),
            pltpu.SemaphoreType.DMA((chunks,)),
            pltpu.SemaphoreType.DMA((2, chunks, group)),
            pltpu.SemaphoreType.DMA((2, chunks, group)),
        ],
        compiler_params=pltpu.CompilerParams(
            collective_id=0, has_side_effects=True, vmem_limit_bytes=40 * 2**20
        ),
        cost_estimate=pl.CostEstimate(
            flops=8 * 14 * chunks * rows * lanes * gdim,
            bytes_accessed=8 * amp_local * 2, transcendentals=0,
        ),
    )(gate_order, gate_starts, pair_gates, x, unitaries)
    y = y.reshape(chunks * rows, 2, lanes).transpose(1, 0, 2)
    return y.reshape(2, amp_local)


def solution(mesh):
    placed = (P(None, ("cuts", "qa")), P(), P(), P(), P())
    return jax.shard_map(
        shards, mesh=mesh, in_specs=placed, out_specs=P(None, ("cuts", "qa")), check_vma=False
    )
```

time: 226 us -> 35.1 us (0.16)
  the two profiles are of different devices: /device:TPU:15 before, /device:TPU:0 now
where the time goes in v1:
time: 35.1 us; the launch traced here: 34.8 us
  Pallas kernels  29.2 us (83%)
  local copies, waits for them, and re-layouts  5.6 us (16%)
    pallas_call x1, Pallas kernels, shards(): pl.pallas_call(functools.partial(kernel, group, unit // lanes), out_shape...  29.2 us
    unnamed x11, local copies, waits for them, and re-layouts  5.6 us

profile of v1, /device:TPU:0, one launch (start us, length us, event | category | flops | bytes accessed | tf_op | source)
XLA Modules:
  0.0 34.8 jit_solution(657680414411504638)
XLA Ops:
  0.0 0.0 copy-start
  0.0 1.4 %copy-done = f32[12,2,128,128]{3,2,1,0:T(8,128)S(1)} copy-done((f32[12,2,128,128]{3,2,1,0:T(8,128)S(1)}, f32[12,2,128,128]{3,2,1,0:T(8,128)}, u32[]{:S(2)}) %copy-start) | copy-done | bytes 1572888
  1.4 0.0 copy-start.1
  1.4 1.2 %copy-done.1 = f32[2,131072]{1,0:T(2,128)S(1)} copy-done((f32[2,131072]{1,0:T(2,128)S(1)}, f32[2,131072]{1,0:T(2,128)}, u32[]{:S(2)}) %copy-start.1) | copy-done | bytes 1048600
  2.6 0.0 copy-start.2
  2.6 0.7 %copy-done.2 = f32[2,2,2,2]{3,2,1,0:T(2,128)S(1)} copy-done((f32[2,2,2,2]{3,2,1,0:T(2,128)S(1)}, f32[2,2,2,2]{3,2,1,0:T(2,128)}, u32[]{:S(2)}) %copy-start.2) | copy-done | bytes 88
  3.3 0.0 copy-start.3
  3.3 0.7 %copy-done.3 = s32[12]{0:T(128)S(1)} copy-done((s32[12]{0:T(128)S(1)}, s32[12]{0:T(128)}, u32[]{:S(2)}) %copy-start.3) | copy-done | bytes 72
  4.0 0.0 copy-start.4
  4.0 0.7 %copy-done.4 = s32[12]{0:T(128)S(1)} copy-done((s32[12]{0:T(128)S(1)}, s32[12]{0:T(128)}, u32[]{:S(2)}) %copy-start.4) | copy-done | bytes 72
  4.6 29.2 %shard_map.55 = f32[4,512,128]{2,1,0:T(8,128)S(1)} custom-call(s32[12]{0:T(128)S(1)} %copy-done.3, s32[12]{0:T(128)S(1)} %copy-done.4, f32[2,2,2,2]{3,2,1,0:T(2,128)S(1)} %copy-done.2, f32[4,512,128]{2,1,0:T(8,128)S(1)} %bitcast.11, f32[12,2,128,128]{3,2,1,0:T(8,128)S(1)} %copy-done), custom_call_target="tpu_custom_call" | custom-call | flops 1879048192 | bytes 2097152 | tf_op jit(solution)/shard_map/pallas_call | solution.py:267
  33.8 1.0 %copy.9 = f32[2,131072]{1,0:T(2,128)} copy(f32[2,131072]{1,0:T(2,128)S(1)} %bitcast.10) | data formatting | bytes 2097152
Async XLA Ops:
  0.0 1.4 %copy-start = (f32[12,2,128,128]{3,2,1,0:T(8,128)S(1)}, f32[12,2,128,128]{3,2,1,0:T(8,128)}, u32[]{:S(2)}) copy-start(f32[12,2,128,128]{3,2,1,0:T(8,128)} %u_hbm.1) | copy-start | bytes 4718596
  1.4 1.2 %copy-start.1 = (f32[2,131072]{1,0:T(2,128)S(1)}, f32[2,131072]{1,0:T(2,128)}, u32[]{:S(2)}) copy-start(f32[2,131072]{1,0:T(2,128)} %param.5) | copy-start | bytes 3145732
  2.6 0.7 %copy-start.2 = (f32[2,2,2,2]{3,2,1,0:T(2,128)S(1)}, f32[2,2,2,2]{3,2,1,0:T(2,128)}, u32[]{:S(2)}) copy-start(f32[2,2,2,2]{3,2,1,0:T(2,128)} %pair.1) | copy-start | bytes 196
  3.3 0.7 %copy-start.3 = (s32[12]{0:T(128)S(1)}, s32[12]{0:T(128)}, u32[]{:S(2)}) copy-start(s32[12]{0:T(128)} %order.1) | copy-start | bytes 148
  4.0 0.7 %copy-start.4 = (s32[12]{0:T(128)S(1)}, s32[12]{0:T(128)}, u32[]{:S(2)}) copy-start(s32[12]{0:T(128)} %starts.1) | copy-start | bytes 148

commit v2 on v1

--- a/solution.py
+++ b/solution.py
@@ -7,6 +7,7 @@
 from jax.experimental.pallas import tpu as pltpu
 from jax.sharding import PartitionSpec as P
 
+VMEM = 63 * 2**20
 BF16 = jnp.bfloat16
 F32 = jnp.float32
 
@@ -121,8 +122,8 @@
 
 
 def kernel(
-    group, pair_bit, order, starts, pair, x_hbm, u_hbm, o_hbm,
-    x_in, u, first_hi, first_lo, plain, woven, w_hi, w_lo,
+    group, pair_bit, order_hbm, starts_hbm, pair_hbm, x_hbm, u_hbm, o_hbm,
+    order, starts, pair, x_in, u, first_hi, first_lo, plain, woven, w_hi, w_lo,
     sent, got, x_out, in_sem, out_sem, send_sem, recv_sem,
 ):
     chunks, rows, lanes = x_in.shape[0], x_in.shape[1] // 2, x_in.shape[2]
@@ -132,17 +133,24 @@
     me = lax.rem(index, group)
     base = index - me
 
+    small = [
+        pltpu.make_async_copy(src, dst, in_sem.at[n])
+        for n, (src, dst) in enumerate(
+            [(order_hbm, order), (starts_hbm, starts), (pair_hbm, pair)]
+        )
+    ]
+    load_u = pltpu.make_async_copy(u_hbm, u, in_sem.at[3])
+    load_x = pltpu.make_async_copy(x_hbm, x_in, in_sem.at[4])
+    for load in small + [load_u, load_x]:
+        load.start()
     barrier = pltpu.get_barrier_semaphore()
     for d in range(1, group):
         pl.semaphore_signal(
             barrier, inc=1, device_id={"qa": base + lax.rem(me + d, group)},
             device_id_type=pl.DeviceIdType.MESH,
         )
-    load_u = pltpu.make_async_copy(u_hbm, u, in_sem.at[0])
-    load_x = pltpu.make_async_copy(x_hbm, x_in, in_sem.at[1])
-    load_u.start()
-    load_x.start()
-    load_u.wait()
+    for load in small + [load_u]:
+        load.wait()
     for k in range(count):
         first_hi[k], first_lo[k] = gate_matrix(u, order, k)
     load_x.wait()
@@ -262,14 +270,16 @@
     group = rows * lanes // unit
     x = state.reshape(2, chunks * rows, lanes).transpose(1, 0, 2)
     x = x.reshape(chunks, 2 * rows, lanes)
-    smem = pl.BlockSpec(memory_space=pltpu.SMEM)
-    hbm = pl.BlockSpec(memory_space=pl.ANY)
+    hbm = pl.BlockSpec(memory_space=pltpu.HBM)
     y = pl.pallas_call(
         functools.partial(kernel, group, unit // lanes),
         out_shape=jax.ShapeDtypeStruct(x.shape, F32),
-        in_specs=[smem, smem, smem, hbm, hbm],
-        out_specs=hbm,
+        in_specs=[hbm] * 5,
+        out_specs=pl.BlockSpec(memory_space=pl.ANY),
         scratch_shapes=[
+            pltpu.SMEM(gate_order.shape, jnp.int32),
+            pltpu.SMEM(gate_starts.shape, jnp.int32),
+            pltpu.SMEM(pair_gates.shape, F32),
             pltpu.VMEM(x.shape, F32),
             pltpu.VMEM(unitaries.shape, F32),
             pltpu.VMEM((ngates // 3, 2 * gdim, 2 * gdim), BF16),
@@ -281,13 +291,13 @@
             pltpu.VMEM((2, chunks, 2, rows, lanes), F32),
             pltpu.VMEM((2, chunks, 2, rows, lanes), F32),
             pltpu.VMEM(x.shape, F32),
-            pltpu.SemaphoreType.DMA((2,)),
+            pltpu.SemaphoreType.DMA((5,)),
             pltpu.SemaphoreType.DMA((chunks,)),
             pltpu.SemaphoreType.DMA((2, chunks, group)),
             pltpu.SemaphoreType.DMA((2, chunks, group)),
         ],
         compiler_params=pltpu.CompilerParams(
-            collective_id=0, has_side_effects=True, vmem_limit_bytes=40 * 2**20
+            collective_id=0, has_side_effects=True, vmem_limit_bytes=VMEM
         ),
         cost_estimate=pl.CostEstimate(
             flops=8 * 14 * chunks * rows * lanes * gdim,

time: 35.1 us -> 33 us (0.940)
  local copies, waits for them, and re-layouts: 5.6 us -> 2.26 us
  Pallas kernels: 29.2 us -> 30.5 us
    unnamed x11 -> x1, local copies, waits for them, and re-layouts: 5.6 us -> 2.26 us
    pallas_call x1, Pallas kernels: 29.2 us -> 30.5 us  [shards(): pl.pallas_call(functools.partial(kernel, group, unit // lanes), out_shape...]
where the time goes in v2:
time: 33 us; the launch traced here: 32.8 us
  Pallas kernels  30.5 us (92%)
  local copies, waits for them, and re-layouts  2.26 us (7%)
    pallas_call x1, Pallas kernels, shards(): pl.pallas_call(functools.partial(kernel, group, unit // lanes), out_shape...  30.5 us
    unnamed x1, local copies, waits for them, and re-layouts  2.26 us

profile of v2, /device:TPU:0, one launch (start us, length us, event | category | flops | bytes accessed | tf_op | source)
XLA Modules:
  0.0 32.8 jit_solution(17658157630518522827)
XLA Ops:
  0.0 30.5 %shard_map.55 = f32[4,512,128]{2,1,0:T(8,128)} custom-call(s32[12]{0:T(128)} %order_hbm.1, s32[12]{0:T(128)} %starts_hbm.1, f32[2,2,2,2]{3,2,1,0:T(2,128)} %pair_hbm.1, f32[4,512,128]{2,1,0:T(8,128)} %bitcast.11, f32[12,2,128,128]{3,2,1,0:T(8,128)} %u_hbm.1), custom_call_target="tpu_custom_call" | custom-call | flops 1879048192 | bytes 2097152 | tf_op jit(solution)/shard_map/pallas_call | solution.py:274
  30.5 2.3 %copy.9 = f32[2,131072]{1,0:T(2,128)} copy(f32[2,131072]{1,0:T(2,128)} %bitcast.10) | data formatting | bytes 2097152

commit v3 on v2

--- a/solution.py
+++ b/solution.py
@@ -7,7 +7,7 @@
 from jax.experimental.pallas import tpu as pltpu
 from jax.sharding import PartitionSpec as P
 
-VMEM = 63 * 2**20
+VMEM = 40 * 2**20
 BF16 = jnp.bfloat16
 F32 = jnp.float32
 
@@ -122,9 +122,9 @@
 
 
 def kernel(
-    group, pair_bit, order_hbm, starts_hbm, pair_hbm, x_hbm, u_hbm, o_hbm,
+    group, pair_bit, order_hbm, starts_hbm, pair_hbm, x_hbm, u_hbm, x_out,
     order, starts, pair, x_in, u, first_hi, first_lo, plain, woven, w_hi, w_lo,
-    sent, got, x_out, in_sem, out_sem, send_sem, recv_sem,
+    sent, got, in_sem, send_sem, recv_sem,
 ):
     chunks, rows, lanes = x_in.shape[0], x_in.shape[1] // 2, x_in.shape[2]
     count = u.shape[0] // 3
@@ -236,21 +236,16 @@
 
     compose(2, count, order, starts, u, plain, woven, w_hi, w_lo, lambda p: p)
 
-    def store(c):
-        return pltpu.make_async_copy(x_out.at[c], o_hbm.at[c], out_sem.at[c])
-
     def last(c, _):
         arrived(1, c)
         y = apply(w_hi, w_lo, got[1, c].reshape(2 * rows, lanes))
         for r in range(2):
             x_out[c, pl.ds(r, rows, stride=2), :] = y[r * rows : (r + 1) * rows]
-        store(c).start()
         return 0
 
     lax.fori_loop(0, chunks, last, 0)
 
     def finish(c, _):
-        store(c).wait()
         for phase in range(2):
             lax.fori_loop(
                 1, group, lambda d, _: (remote(phase, c, d).wait_send(), 0)[1], 0
@@ -273,9 +268,9 @@
     hbm = pl.BlockSpec(memory_space=pltpu.HBM)
     y = pl.pallas_call(
         functools.partial(kernel, group, unit // lanes),
-        out_shape=jax.ShapeDtypeStruct(x.shape, F32),
+        out_shape=pltpu.VMEM(x.shape, F32),
         in_specs=[hbm] * 5,
-        out_specs=pl.BlockSpec(memory_space=pl.ANY),
+        out_specs=pl.BlockSpec(memory_space=pltpu.VMEM),
         scratch_shapes=[
             pltpu.SMEM(gate_order.shape, jnp.int32),
             pltpu.SMEM(gate_starts.shape, jnp.int32),
@@ -290,9 +285,7 @@
             pltpu.VMEM((2 * rows, 2 * rows), BF16),
             pltpu.VMEM((2, chunks, 2, rows, lanes), F32),
             pltpu.VMEM((2, chunks, 2, rows, lanes), F32),
-            pltpu.VMEM(x.shape, F32),
             pltpu.SemaphoreType.DMA((5,)),
-            pltpu.SemaphoreType.DMA((chunks,)),
             pltpu.SemaphoreType.DMA((2, chunks, group)),
             pltpu.SemaphoreType.DMA((2, chunks, group)),
         ],
@@ -303,7 +296,10 @@
             flops=8 * 14 * chunks * rows * lanes * gdim,
             bytes_accessed=8 * amp_local * 2, transcendentals=0,
         ),
-    )(gate_order, gate_starts, pair_gates, x, unitaries)
+    )(*(
+        pltpu.with_memory_space_constraint(a, pltpu.HBM)
+        for a in (gate_order, gate_starts, pair_gates, x, unitaries)
+    ))
     y = y.reshape(chunks * rows, 2, lanes).transpose(1, 0, 2)
     return y.reshape(2, amp_local)
 

time: 33 us -> 31.1 us (0.942)
  local copies, waits for them, and re-layouts: 2.26 us -> 0.97 us
  Pallas kernels: 30.5 us -> 29.9 us
    unnamed x1, local copies, waits for them, and re-layouts: 2.26 us -> 0.97 us
    pallas_call x1, Pallas kernels: 30.5 us -> 29.9 us  [shards(): pl.pallas_call(functools.partial(kernel, group, unit // lanes), out_shape...]
where the time goes in v3:
time: 31.1 us; the launch traced here: 30.9 us
  Pallas kernels  29.9 us (96%)
  local copies, waits for them, and re-layouts  0.97 us (3%)
    pallas_call x1, Pallas kernels, shards(): pl.pallas_call(functools.partial(kernel, group, unit // lanes), out_shape...  29.9 us
    unnamed x1, local copies, waits for them, and re-layouts  0.97 us

profile of v3, /device:TPU:0, one launch (start us, length us, event | category | flops | bytes accessed | tf_op | source)
XLA Modules:
  0.0 30.9 jit_solution(6177591695118063036)
XLA Ops:
  0.0 29.9 %shard_map.55 = f32[4,512,128]{2,1,0:T(8,128)S(1)} custom-call(s32[12]{0:T(128)} %order_hbm.1, s32[12]{0:T(128)} %starts_hbm.1, f32[2,2,2,2]{3,2,1,0:T(2,128)} %pair_hbm.1, f32[4,512,128]{2,1,0:T(8,128)} %bitcast.11, f32[12,2,128,128]{3,2,1,0:T(8,128)} %u_hbm.1), custom_call_target="tpu_custom_call" | custom-call | flops 1879048192 | bytes 2097152 | tf_op jit(solution)/shard_map/pallas_call | solution.py:269
  29.9 1.0 %copy.9 = f32[2,131072]{1,0:T(2,128)} copy(f32[2,131072]{1,0:T(2,128)S(1)} %bitcast.10) | data formatting | bytes 2097152

commit v4 on v3

--- a/solution.py
+++ b/solution.py
@@ -90,7 +90,7 @@
 
 
 def compose(third, count, order, starts, u, plain, woven, w_hi, w_lo, after):
-    rows, lanes = plain.shape[1], plain.shape[2]
+    rows, lanes = plain.shape[2], plain.shape[3]
     ks = [third * count + j for j in range(count)]
     built = [gate_matrix(u, order, k) for k in ks]
     for n in range(rows // lanes):
@@ -101,8 +101,8 @@
             [one, jnp.zeros_like(one)],
             [lambda m=m: m for m in built],
             [starts[k] for k in ks],
-            plain,
-            woven,
+            plain.at[n],
+            woven.at[n],
         )
         re, im = after(planes)
         for out, r, i in zip((w_hi, w_lo), split(re), split(im)):
@@ -124,14 +124,17 @@
 def kernel(
     group, pair_bit, order_hbm, starts_hbm, pair_hbm, x_hbm, u_hbm, x_out,
     order, starts, pair, x_in, u, first_hi, first_lo, plain, woven, w_hi, w_lo,
-    sent, got, in_sem, send_sem, recv_sem,
+    sent, got, raw_got, mid_sent, mid_got, back, final,
+    in_sem, send_sem, recv_sem, mid_send, mid_recv, raw_send, raw_recv,
 ):
     chunks, rows, lanes = x_in.shape[0], x_in.shape[1] // 2, x_in.shape[2]
     count = u.shape[0] // 3
     block = rows // group
+    half, sub_group = chunks // 2, group // 2
     index = lax.axis_index("qa")
     me = lax.rem(index, group)
     base = index - me
+    top, sub = me // sub_group, lax.rem(me, sub_group)
 
     small = [
         pltpu.make_async_copy(src, dst, in_sem.at[n])
@@ -141,77 +144,123 @@
     ]
     load_u = pltpu.make_async_copy(u_hbm, u, in_sem.at[3])
     load_x = pltpu.make_async_copy(x_hbm, x_in, in_sem.at[4])
-    for load in small + [load_u, load_x]:
-        load.start()
     barrier = pltpu.get_barrier_semaphore()
     for d in range(1, group):
         pl.semaphore_signal(
             barrier, inc=1, device_id={"qa": base + lax.rem(me + d, group)},
             device_id_type=pl.DeviceIdType.MESH,
         )
+    for load in small + [load_u, load_x]:
+        load.start()
+
+    def copy_to(peer, src, dst, send, recv):
+        return pltpu.make_async_remote_copy(
+            src_ref=src, dst_ref=dst, send_sem=send, recv_sem=recv,
+            device_id={"qa": base + peer}, device_id_type=pl.DeviceIdType.MESH,
+        )
+
+    partner = lax.rem(me + sub_group, group)
+    raw = copy_to(
+        partner, x_hbm.at[(1 - top) * half], raw_got, raw_send.at[0], raw_recv.at[0]
+    )
+    ret = copy_to(partner, back, final.at[top], raw_send.at[1], raw_recv.at[1])
+
+    def block_at(j):
+        return pl.ds(pl.multiple_of(j * block, block), block)
+
+    def remote(phase, c, d):
+        peer = lax.rem(me + d, group)
+        return copy_to(
+            peer,
+            sent.at[phase, c, :, block_at(peer), :],
+            got.at[phase, c, :, block_at(me), :],
+            send_sem.at[phase, c, d],
+            recv_sem.at[phase, c, d],
+        )
+
+    def exchange(phase, c):
+        def one(d, _):
+            remote(phase, c, d).start()
+            return 0
+
+        lax.fori_loop(1, group, one, 0)
+        got[phase, c, :, block_at(me), :] = sent[phase, c, :, block_at(me), :]
+
+    def arrived(phase, c):
+        def one(d, _):
+            remote(phase, c, d).wait_recv()
+            return 0
+
+        lax.fori_loop(1, group, one, 0)
+
+    def middle(phase, d):
+        peer = lax.rem(sub + d, sub_group)
+        return copy_to(
+            top * sub_group + peer,
+            mid_sent.at[phase, :, block_at(peer), :],
+            mid_got.at[phase, :, block_at(sub), :],
+            mid_send.at[phase, d],
+            mid_recv.at[phase, d],
+        )
+
+    def middle_exchange(phase):
+        def one(d, _):
+            middle(phase, d).start()
+            return 0
+
+        lax.fori_loop(1, sub_group, one, 0)
+        mid_got[phase, :, block_at(sub), :] = mid_sent[phase, :, block_at(sub), :]
+
+    def middle_arrived(phase):
+        def one(d, _):
+            middle(phase, d).wait_recv()
+            return 0
+
+        lax.fori_loop(1, sub_group, one, 0)
+
+    def first_third(planes):
+        return run_gates(
+            planes,
+            [lambda k=k: (first_hi[k], first_lo[k]) for k in range(count)],
+            [starts[k] for k in range(count)],
+            plain.at[0],
+            woven.at[0],
+        )
+
+    def planes_of(ref):
+        return [ref[pl.ds(r, rows, stride=2), :] for r in range(2)]
+
+    pl.semaphore_wait(barrier, group - 1)
+    raw.start()
     for load in small + [load_u]:
         load.wait()
     for k in range(count):
         first_hi[k], first_lo[k] = gate_matrix(u, order, k)
     load_x.wait()
 
-    def block_at(j):
-        return pl.ds(pl.multiple_of(j * block, block), block)
-
-    def remote(phase, c, d):
-        peer = lax.rem(me + d, group)
-        return pltpu.make_async_remote_copy(
-            src_ref=sent.at[phase, c, :, block_at(peer), :],
-            dst_ref=got.at[phase, c, :, block_at(me), :],
-            send_sem=send_sem.at[phase, c, d],
-            recv_sem=recv_sem.at[phase, c, d],
-            device_id={"qa": base + peer},
-            device_id_type=pl.DeviceIdType.MESH,
-        )
-
-    def exchange(phase, c):
-        def one(d, _):
-            remote(phase, c, d).start()
-            return 0
-
-        lax.fori_loop(1, group, one, 0)
-        got[phase, c, :, block_at(me), :] = sent[phase, c, :, block_at(me), :]
-
-    def arrived(phase, c):
-        def one(d, _):
-            remote(phase, c, d).wait_recv()
-            return 0
-
-        lax.fori_loop(1, group, one, 0)
-
-    def first_gates(c):
-        half = chunks // 2
-        low, high = lax.rem(c, half), lax.rem(c, half) + half
-
-        def planes_of(n):
-            return [x_in[n, pl.ds(r, rows, stride=2), :] for r in range(2)]
-
-        planes = mix_pair(pair, 0, c // half, planes_of(low), planes_of(high))
-        done = run_gates(
-            planes,
-            [lambda k=k: (first_hi[k], first_lo[k]) for k in range(count)],
-            [starts[k] for k in range(count)],
-            plain,
-            woven,
+    others = [c for c in range(chunks) if c % half]
+
+    def first(i, _):
+        b, low = i // (half - 1), 1 + lax.rem(i, half - 1)
+        c = b * half + low
+        done = first_third(
+            mix_pair(pair, 0, b, planes_of(x_in.at[low]), planes_of(x_in.at[low + half]))
         )
         for r in range(2):
             sent[0, c, r] = done[r]
-
-    first_gates(jnp.int32(0))
-    pl.semaphore_wait(barrier, group - 1)
-    exchange(0, jnp.int32(0))
-
-    def first(c, _):
-        first_gates(c)
         exchange(0, c)
         return 0
 
-    lax.fori_loop(1, chunks, first, 0)
+    lax.fori_loop(0, len(others), first, 0)
+
+    def first_raw(source, ref):
+        done = first_third(planes_of(ref))
+        for s in range(2):
+            for r in range(2):
+                part = done[r][s * rows // 2 : (s + 1) * rows // 2]
+                mid_sent[0, s * 4 + r * 2 + source] = part
+
+    first_raw(top, x_in.at[top * half])
 
     def with_pair(planes):
         pieces = ([], [])
@@ -225,34 +274,62 @@
 
     compose(1, count, order, starts, u, plain, woven, w_hi, w_lo, with_pair)
 
-    def second(c, _):
+    def second(c):
         arrived(0, c)
         y = apply(w_hi, w_lo, got[0, c].reshape(2 * rows, lanes))
         sent[1, c] = y.reshape(2, rows, lanes)
         exchange(1, c)
-        return 0
-
-    lax.fori_loop(0, chunks, second, 0)
+
+    early = len(others) // 2
+    for c in others[:early]:
+        second(c)
+    raw.wait_recv()
+    first_raw(1 - top, raw_got)
+    middle_exchange(0)
+    for c in others[early:]:
+        second(c)
+    middle_arrived(0)
+    for s in range(2):
+        here = slice(4 * s, 4 * s + 4)
+        y = apply(w_hi, w_lo, mid_got[0, here].reshape(2 * rows, lanes))
+        mid_sent[1, here] = y.reshape(4, rows // 2, lanes)
+    middle_exchange(1)
 
     compose(2, count, order, starts, u, plain, woven, w_hi, w_lo, lambda p: p)
 
-    def last(c, _):
+    middle_arrived(1)
+
+    def last_raw(source):
+        parts = [mid_got[1, s * 4 + r * 2 + source] for r in range(2) for s in range(2)]
+        y = apply(w_hi, w_lo, jnp.concatenate(parts, axis=0))
+        return y.reshape(2, rows, lanes)
+
+    back[...] = last_raw(1 - top)
+    ret.start()
+    final[top] = last_raw(top)
+
+    for c in others:
         arrived(1, c)
         y = apply(w_hi, w_lo, got[1, c].reshape(2 * rows, lanes))
         for r in range(2):
             x_out[c, pl.ds(r, rows, stride=2), :] = y[r * rows : (r + 1) * rows]
-        return 0
-
-    lax.fori_loop(0, chunks, last, 0)
-
-    def finish(c, _):
-        for phase in range(2):
+
+    ret.wait_recv()
+    for b in range(2):
+        low, high = [[final[n, r] for r in range(2)] for n in range(2)]
+        for r, plane in enumerate(mix_pair(pair, 0, b, low, high)):
+            x_out[b * half, pl.ds(r, rows, stride=2), :] = plane
+
+    raw.wait_send()
+    ret.wait_send()
+    for phase in range(2):
+        lax.fori_loop(
+            1, sub_group, lambda d, _: (middle(phase, d).wait_send(), 0)[1], 0
+        )
+        for c in others:
             lax.fori_loop(
                 1, group, lambda d, _: (remote(phase, c, d).wait_send(), 0)[1], 0
             )
-        return 0
-
-    lax.fori_loop(0, chunks, finish, 0)
 
 
 def shards(state, unitaries, gate_order, gate_starts, pair_gates):
@@ -279,15 +356,24 @@
             pltpu.VMEM(unitaries.shape, F32),
             pltpu.VMEM((ngates // 3, 2 * gdim, 2 * gdim), BF16),
             pltpu.VMEM((ngates // 3, 2 * gdim, 2 * gdim), BF16),
-            pltpu.VMEM((2, rows, lanes), F32),
-            pltpu.VMEM((2, rows, lanes), F32),
+            pltpu.VMEM((rows // lanes, 2, rows, lanes), F32),
+            pltpu.VMEM((rows // lanes, 2, rows, lanes), F32),
             pltpu.VMEM((2 * rows, 2 * rows), BF16),
             pltpu.VMEM((2 * rows, 2 * rows), BF16),
             pltpu.VMEM((2, chunks, 2, rows, lanes), F32),
             pltpu.VMEM((2, chunks, 2, rows, lanes), F32),
+            pltpu.VMEM((2 * rows, lanes), F32),
+            pltpu.VMEM((2, 8, rows // 2, lanes), F32),
+            pltpu.VMEM((2, 8, rows // 2, lanes), F32),
+            pltpu.VMEM((2, rows, lanes), F32),
+            pltpu.VMEM((2, 2, rows, lanes), F32),
             pltpu.SemaphoreType.DMA((5,)),
             pltpu.SemaphoreType.DMA((2, chunks, group)),
             pltpu.SemaphoreType.DMA((2, chunks, group)),
+            pltpu.SemaphoreType.DMA((2, group // 2)),
+            pltpu.SemaphoreType.DMA((2, group // 2)),
+            pltpu.SemaphoreType.DMA((2,)),
+            pltpu.SemaphoreType.DMA((2,)),
         ],
         compiler_params=pltpu.CompilerParams(
             collective_id=0, has_side_effects=True, vmem_limit_bytes=VMEM

time: 31.1 us -> 30.8 us (level)
  no operation moved by 1% of the time
where the time goes in v4:
time: 30.8 us; the launch traced here: 30.6 us
  Pallas kernels  29.7 us (96%)
  local copies, waits for them, and re-layouts  0.97 us (3%)
    pallas_call x1, Pallas kernels, shards(): pl.pallas_call(functools.partial(kernel, group, unit // lanes), out_shape...  29.7 us
    unnamed x1, local copies, waits for them, and re-layouts  0.97 us

profile of v4, /device:TPU:0, one launch (start us, length us, event | category | flops | bytes accessed | tf_op | source)
XLA Modules:
  0.0 30.6 jit_solution(11116946274937740450)
XLA Ops:
  0.0 29.7 %shard_map.55 = f32[4,512,128]{2,1,0:T(8,128)S(1)} custom-call(s32[12]{0:T(128)} %order_hbm.1, s32[12]{0:T(128)} %starts_hbm.1, f32[2,2,2,2]{3,2,1,0:T(2,128)} %pair_hbm.1, f32[4,512,128]{2,1,0:T(8,128)} %bitcast.11, f32[12,2,128,128]{3,2,1,0:T(8,128)} %u_hbm.1), custom_call_target="tpu_custom_call" | custom-call | flops 1879048192 | bytes 2097152 | tf_op jit(solution)/shard_map/pallas_call | solution.py:346
  29.7 1.0 %copy.9 = f32[2,131072]{1,0:T(2,128)} copy(f32[2,131072]{1,0:T(2,128)S(1)} %bitcast.10) | data formatting | bytes 2097152

commit v5 on v4

--- a/solution.py
+++ b/solution.py
@@ -193,27 +193,29 @@
 
         lax.fori_loop(1, group, one, 0)
 
-    def middle(phase, d):
+    def middle(phase, s, d):
         peer = lax.rem(sub + d, sub_group)
+        here = pl.ds(4 * s, 4)
         return copy_to(
             top * sub_group + peer,
-            mid_sent.at[phase, :, block_at(peer), :],
-            mid_got.at[phase, :, block_at(sub), :],
-            mid_send.at[phase, d],
-            mid_recv.at[phase, d],
-        )
-
-    def middle_exchange(phase):
+            mid_sent.at[phase, here, block_at(peer), :],
+            mid_got.at[phase, here, block_at(sub), :],
+            mid_send.at[phase, s, d],
+            mid_recv.at[phase, s, d],
+        )
+
+    def middle_exchange(phase, s):
         def one(d, _):
-            middle(phase, d).start()
+            middle(phase, s, d).start()
             return 0
 
         lax.fori_loop(1, sub_group, one, 0)
-        mid_got[phase, :, block_at(sub), :] = mid_sent[phase, :, block_at(sub), :]
-
-    def middle_arrived(phase):
+        here = slice(4 * s, 4 * s + 4)
+        mid_got[phase, here, block_at(sub), :] = mid_sent[phase, here, block_at(sub), :]
+
+    def middle_arrived(phase, s):
         def one(d, _):
-            middle(phase, d).wait_recv()
+            middle(phase, s, d).wait_recv()
             return 0
 
         lax.fori_loop(1, sub_group, one, 0)
@@ -272,11 +274,12 @@
                     out.append(part)
         return [jnp.concatenate(p, axis=0) for p in pieces]
 
-    compose(1, count, order, starts, u, plain, woven, w_hi, w_lo, with_pair)
+    compose(1, count, order, starts, u, plain, woven, w_hi.at[0], w_lo.at[0], with_pair)
+    compose(2, count, order, starts, u, plain, woven, w_hi.at[1], w_lo.at[1], lambda p: p)
 
     def second(c):
         arrived(0, c)
-        y = apply(w_hi, w_lo, got[0, c].reshape(2 * rows, lanes))
+        y = apply(w_hi.at[0], w_lo.at[0], got[0, c].reshape(2 * rows, lanes))
         sent[1, c] = y.reshape(2, rows, lanes)
         exchange(1, c)
 
@@ -285,23 +288,23 @@
         second(c)
     raw.wait_recv()
     first_raw(1 - top, raw_got)
-    middle_exchange(0)
+    for s in range(2):
+        middle_exchange(0, s)
     for c in others[early:]:
         second(c)
-    middle_arrived(0)
     for s in range(2):
+        middle_arrived(0, s)
         here = slice(4 * s, 4 * s + 4)
-        y = apply(w_hi, w_lo, mid_got[0, here].reshape(2 * rows, lanes))
+        y = apply(w_hi.at[0], w_lo.at[0], mid_got[0, here].reshape(2 * rows, lanes))
         mid_sent[1, here] = y.reshape(4, rows // 2, lanes)
-    middle_exchange(1)
-
-    compose(2, count, order, starts, u, plain, woven, w_hi, w_lo, lambda p: p)
-
-    middle_arrived(1)
+        middle_exchange(1, s)
+
+    for s in range(2):
+        middle_arrived(1, s)
 
     def last_raw(source):
         parts = [mid_got[1, s * 4 + r * 2 + source] for r in range(2) for s in range(2)]
-        y = apply(w_hi, w_lo, jnp.concatenate(parts, axis=0))
+        y = apply(w_hi.at[1], w_lo.at[1], jnp.concatenate(parts, axis=0))
         return y.reshape(2, rows, lanes)
 
     back[...] = last_raw(1 - top)
@@ -310,7 +313,7 @@
 
     for c in others:
         arrived(1, c)
-        y = apply(w_hi, w_lo, got[1, c].reshape(2 * rows, lanes))
+        y = apply(w_hi.at[1], w_lo.at[1], got[1, c].reshape(2 * rows, lanes))
         for r in range(2):
             x_out[c, pl.ds(r, rows, stride=2), :] = y[r * rows : (r + 1) * rows]
 
@@ -323,9 +326,10 @@
     raw.wait_send()
     ret.wait_send()
     for phase in range(2):
-        lax.fori_loop(
-            1, sub_group, lambda d, _: (middle(phase, d).wait_send(), 0)[1], 0
-        )
+        for s in range(2):
+            lax.fori_loop(
+                1, sub_group, lambda d, _: (middle(phase, s, d).wait_send(), 0)[1], 0
+            )
         for c in others:
             lax.fori_loop(
                 1, group, lambda d, _: (remote(phase, c, d).wait_send(), 0)[1], 0
@@ -358,8 +362,8 @@
             pltpu.VMEM((ngates // 3, 2 * gdim, 2 * gdim), BF16),
             pltpu.VMEM((rows // lanes, 2, rows, lanes), F32),
             pltpu.VMEM((rows // lanes, 2, rows, lanes), F32),
-            pltpu.VMEM((2 * rows, 2 * rows), BF16),
-            pltpu.VMEM((2 * rows, 2 * rows), BF16),
+            pltpu.VMEM((2, 2 * rows, 2 * rows), BF16),
+            pltpu.VMEM((2, 2 * rows, 2 * rows), BF16),
             pltpu.VMEM((2, chunks, 2, rows, lanes), F32),
             pltpu.VMEM((2, chunks, 2, rows, lanes), F32),
             pltpu.VMEM((2 * rows, lanes), F32),
@@ -370,8 +374,8 @@
             pltpu.SemaphoreType.DMA((5,)),
             pltpu.SemaphoreType.DMA((2, chunks, group)),
             pltpu.SemaphoreType.DMA((2, chunks, group)),
-            pltpu.SemaphoreType.DMA((2, group // 2)),
-            pltpu.SemaphoreType.DMA((2, group // 2)),
+            pltpu.SemaphoreType.DMA((2, 2, group // 2)),
+            pltpu.SemaphoreType.DMA((2, 2, group // 2)),
             pltpu.SemaphoreType.DMA((2,)),
             pltpu.SemaphoreType.DMA((2,)),
         ],

time: 30.8 us -> 29.5 us (0.958)
  Pallas kernels: 29.7 us -> 28.4 us
    pallas_call x1, Pallas kernels: 29.7 us -> 28.4 us  [shards(): pl.pallas_call(functools.partial(kernel, group, unit // lanes), out_shape...]
where the time goes in v5:
time: 29.5 us; the launch traced here: 29.4 us
  Pallas kernels  28.4 us (96%)
  local copies, waits for them, and re-layouts  0.97 us (3%)
    pallas_call x1, Pallas kernels, shards(): pl.pallas_call(functools.partial(kernel, group, unit // lanes), out_shape...  28.4 us
    unnamed x1, local copies, waits for them, and re-layouts  0.97 us

profile of v5, /device:TPU:0, one launch (start us, length us, event | category | flops | bytes accessed | tf_op | source)
XLA Modules:
  0.0 29.4 jit_solution(14812001357762285354)
XLA Ops:
  0.0 28.4 %shard_map.55 = f32[4,512,128]{2,1,0:T(8,128)S(1)} custom-call(s32[12]{0:T(128)} %order_hbm.1, s32[12]{0:T(128)} %starts_hbm.1, f32[2,2,2,2]{3,2,1,0:T(2,128)} %pair_hbm.1, f32[4,512,128]{2,1,0:T(8,128)} %bitcast.11, f32[12,2,128,128]{3,2,1,0:T(8,128)} %u_hbm.1), custom_call_target="tpu_custom_call" | custom-call | flops 1879048192 | bytes 2097152 | tf_op jit(solution)/shard_map/pallas_call | solution.py:350
  28.4 1.0 %copy.9 = f32[2,131072]{1,0:T(2,128)} copy(f32[2,131072]{1,0:T(2,128)S(1)} %bitcast.10) | data formatting | bytes 2097152

commit v6 on v5

--- a/solution.py
+++ b/solution.py
@@ -30,13 +30,14 @@
 def gate_matrix(u, order, k):
     re_hi, re_lo = split(u[order[k], 0])
     im_hi, im_lo = split(u[order[k], 1])
-    return embed(re_hi, im_hi), embed(re_lo, im_lo)
+    return jnp.concatenate([embed(re_hi, im_hi), embed(re_lo, im_lo)], axis=0)
 
 
 def product(mat, x):
-    hi, lo = mat
+    size = mat.shape[1]
     x_hi, x_lo = split(x)
-    return dot(hi, x_hi) + dot(hi, x_lo) + dot(lo, x_hi)
+    both = dot(mat, x_hi)
+    return both[:size] + both[size:] + dot(mat[:size], x_lo)
 
 
 def relayout(y, plain, woven, old, new):
@@ -89,23 +90,26 @@
     return re, im
 
 
-def compose(third, count, order, starts, u, plain, woven, w_hi, w_lo, after):
-    rows, lanes = plain.shape[2], plain.shape[3]
+def compose(third, count, n, order, starts, u, plain, woven, after):
+    rows, lanes = plain.shape[1], plain.shape[2]
     ks = [third * count + j for j in range(count)]
-    built = [gate_matrix(u, order, k) for k in ks]
-    for n in range(rows // lanes):
-        at = lax.broadcasted_iota(jnp.int32, (rows, lanes), 0)
-        col = lax.broadcasted_iota(jnp.int32, (rows, lanes), 1) + n * lanes
-        one = jnp.where(at == col, 1.0, 0.0).astype(F32)
-        planes = run_gates(
-            [one, jnp.zeros_like(one)],
-            [lambda m=m: m for m in built],
-            [starts[k] for k in ks],
-            plain.at[n],
-            woven.at[n],
-        )
-        re, im = after(planes)
-        for out, r, i in zip((w_hi, w_lo), split(re), split(im)):
+    at = lax.broadcasted_iota(jnp.int32, (rows, lanes), 0)
+    col = lax.broadcasted_iota(jnp.int32, (rows, lanes), 1) + n * lanes
+    one = jnp.where(at == col, 1.0, 0.0).astype(F32)
+    planes = run_gates(
+        [one, jnp.zeros_like(one)],
+        [lambda k=k: gate_matrix(u, order, k) for k in ks],
+        [starts[k] for k in ks],
+        plain,
+        woven,
+    )
+    return after(planes)
+
+
+def place(columns, w_hi, w_lo):
+    blocks, _, rows, lanes = columns.shape
+    for n in range(blocks):
+        for out, r, i in zip((w_hi, w_lo), split(columns[n, 0]), split(columns[n, 1])):
             here = slice(n * lanes, (n + 1) * lanes)
             there = slice(rows + n * lanes, rows + (n + 1) * lanes)
             out[:rows, here] = r
@@ -123,9 +127,10 @@
 
 def kernel(
     group, pair_bit, order_hbm, starts_hbm, pair_hbm, x_hbm, u_hbm, x_out,
-    order, starts, pair, x_in, u, first_hi, first_lo, plain, woven, w_hi, w_lo,
+    order, starts, pair, x_in, u, first_mat, columns, plain, woven, w_hi, w_lo,
     sent, got, raw_got, mid_sent, mid_got, back, final,
     in_sem, send_sem, recv_sem, mid_send, mid_recv, raw_send, raw_recv,
+    share_send, share_recv,
 ):
     chunks, rows, lanes = x_in.shape[0], x_in.shape[1] // 2, x_in.shape[2]
     count = u.shape[0] // 3
@@ -223,10 +228,10 @@
     def first_third(planes):
         return run_gates(
             planes,
-            [lambda k=k: (first_hi[k], first_lo[k]) for k in range(count)],
+            [lambda k=k: first_mat[k] for k in range(count)],
             [starts[k] for k in range(count)],
-            plain.at[0],
-            woven.at[0],
+            plain,
+            woven,
         )
 
     def planes_of(ref):
@@ -237,7 +242,7 @@
     for load in small + [load_u]:
         load.wait()
     for k in range(count):
-        first_hi[k], first_lo[k] = gate_matrix(u, order, k)
+        first_mat[k] = gate_matrix(u, order, k)
     load_x.wait()
 
     others = [c for c in range(chunks) if c % half]
@@ -274,8 +279,25 @@
                     out.append(part)
         return [jnp.concatenate(p, axis=0) for p in pieces]
 
-    compose(1, count, order, starts, u, plain, woven, w_hi.at[0], w_lo.at[0], with_pair)
-    compose(2, count, order, starts, u, plain, woven, w_hi.at[1], w_lo.at[1], lambda p: p)
+    mine = lax.rem(me, 2)
+    shares = [
+        copy_to(
+            me + 1 - 2 * mine, columns.at[t, mine], columns.at[t, mine],
+            share_send.at[t], share_recv.at[t],
+        )
+        for t in range(2)
+    ]
+    for t, after in enumerate((with_pair, lambda p: p)):
+        planes = compose(1 + t, count, mine, order, starts, u, plain, woven, after)
+        for r in range(2):
+            columns[t, mine, r] = planes[r]
+        shares[t].start()
+
+    def placed(t):
+        shares[t].wait_recv()
+        place(columns.at[t], w_hi.at[t], w_lo.at[t])
+
+    placed(0)
 
     def second(c):
         arrived(0, c)
@@ -286,6 +308,7 @@
     early = len(others) // 2
     for c in others[:early]:
         second(c)
+    placed(1)
     raw.wait_recv()
     first_raw(1 - top, raw_got)
     for s in range(2):
@@ -323,6 +346,8 @@
         for r, plane in enumerate(mix_pair(pair, 0, b, low, high)):
             x_out[b * half, pl.ds(r, rows, stride=2), :] = plane
 
+    for share in shares:
+        share.wait_send()
     raw.wait_send()
     ret.wait_send()
     for phase in range(2):
@@ -358,10 +383,10 @@
             pltpu.SMEM(pair_gates.shape, F32),
             pltpu.VMEM(x.shape, F32),
             pltpu.VMEM(unitaries.shape, F32),
-            pltpu.VMEM((ngates // 3, 2 * gdim, 2 * gdim), BF16),
-            pltpu.VMEM((ngates // 3, 2 * gdim, 2 * gdim), BF16),
-            pltpu.VMEM((rows // lanes, 2, rows, lanes), F32),
-            pltpu.VMEM((rows // lanes, 2, rows, lanes), F32),
+            pltpu.VMEM((ngates // 3, 4 * gdim, 2 * gdim), BF16),
+            pltpu.VMEM((2, 2, 2, rows, lanes), F32),
+            pltpu.VMEM((2, rows, lanes), F32),
+            pltpu.VMEM((2, rows, lanes), F32),
             pltpu.VMEM((2, 2 * rows, 2 * rows), BF16),
             pltpu.VMEM((2, 2 * rows, 2 * rows), BF16),
             pltpu.VMEM((2, chunks, 2, rows, lanes), F32),
@@ -378,6 +403,8 @@
             pltpu.SemaphoreType.DMA((2, 2, group // 2)),
             pltpu.SemaphoreType.DMA((2,)),
             pltpu.SemaphoreType.DMA((2,)),
+            pltpu.SemaphoreType.DMA((2,)),
+            pltpu.SemaphoreType.DMA((2,)),
         ],
         compiler_params=pltpu.CompilerParams(
             collective_id=0, has_side_effects=True, vmem_limit_bytes=VMEM

time: 29.5 us -> 29.5 us (level)
  no operation moved by 1% of the time
where the time goes in v6:
time: 29.5 us; the launch traced here: 29.3 us
  Pallas kernels  28.4 us (96%)
  local copies, waits for them, and re-layouts  0.97 us (3%)
    pallas_call x1, Pallas kernels, shards(): pl.pallas_call(functools.partial(kernel, group, unit // lanes), out_shape...  28.4 us
    unnamed x1, local copies, waits for them, and re-layouts  0.97 us

profile of v6, /device:TPU:0, one launch (start us, length us, event | category | flops | bytes accessed | tf_op | source)
XLA Modules:
  0.0 29.3 jit_solution(10426978030049538343)
XLA Ops:
  0.0 28.4 %shard_map.55 = f32[4,512,128]{2,1,0:T(8,128)S(1)} custom-call(s32[12]{0:T(128)} %order_hbm.1, s32[12]{0:T(128)} %starts_hbm.1, f32[2,2,2,2]{3,2,1,0:T(2,128)} %pair_hbm.1, f32[4,512,128]{2,1,0:T(8,128)} %bitcast.11, f32[12,2,128,128]{3,2,1,0:T(8,128)} %u_hbm.1), custom_call_target="tpu_custom_call" | custom-call | flops 1879048192 | bytes 2097152 | tf_op jit(solution)/shard_map/pallas_call | solution.py:375
  28.4 1.0 %copy.9 = f32[2,131072]{1,0:T(2,128)} copy(f32[2,131072]{1,0:T(2,128)S(1)} %bitcast.10) | data formatting | bytes 2097152
